TPU v7x, 512 devices: a whole 4x4x16 slice. The times are simulated.
512 devices in a mesh: pair: 64 (over x, z), virt: 8 (over y, core).
Axes of the slice: x: 4, y: 4, z: 16, core: 2. Of those that a mesh axis runs over, the one named last changes fastest.
Arguments:
- amplitudes: float32 [128, 512, 512], P('pair', 'virt'), may hold values from -6 to 6
- integral_store: float32 [8, 64, 128, 128], P('virt', 'pair'), may hold values from -0.1875 to 0.1875
- domains: int32 [128, 4], P('pair'), may hold values from 0 to 7, as said below
- domain_length: int32 [128], P('pair'), may hold values from 1 to 4
- owner_map: int32 [64], replicated, may hold values from 0 to 63, each once
Outputs:
- ladder: float32 [128, 512, 512], P('pair', 'virt')
Inputs may be any that keep to these rules, and one draw needn't show every extreme that they name: `domains`: each row names 4 different tiles; only the first domain_length entries of a row are live.
All inputs are finite; a program needn't handle non-finite values.
Results may differ from a plain program's by a relative error of at most 0.000098.
Values sent between devices are 32-bit elements; how exact they have to be, the bound alone decides.
No kernel may reach another device: no remote copies, remote signals or barrier semaphores. Data moves between devices by JAX's collectives and lax.ppermute only.
A program may use at most 64 MiB of HBM per device.

v0:
```python
import jax
import jax.numpy as jnp
from jax import lax
from jax.sharding import PartitionSpec as P

TILE = 128
M = 4
NT = 8


def ladder_term(matrix, masked):
    half = jnp.einsum("qrc,cd->qrd", matrix, masked, precision=lax.Precision.HIGHEST)
    return jnp.einsum("qrd,qbd->rb", half, matrix, precision=lax.Precision.HIGHEST)


def on_device(amplitudes, integral_store, domains, domain_length, owner_map):
    order = M * TILE
    full_amps = lax.all_gather(amplitudes, "virt", axis=1, tiled=True)
    whole_store = lax.all_gather(integral_store, "pair", axis=1, tiled=True)
    local_q = integral_store.shape[0]
    pairs = amplitudes.shape[0]
    live = (jnp.arange(M)[None, :] < domain_length[:, None]).astype(jnp.float32)
    position = owner_map[domains[:, :, None] * NT + domains[:, None, :]]
    picked = jnp.take(whole_store, position.reshape(-1), axis=1)
    picked = picked.reshape(local_q, pairs, M, M, TILE, TILE)
    picked = picked * (live[:, :, None] * live[:, None, :])[None, :, :, :, None, None]
    matrices = picked.transpose(1, 0, 2, 4, 3, 5).reshape(pairs, local_q, order, order)
    row_live = jnp.repeat(live, TILE, axis=1)
    masked = full_amps * row_live[:, :, None] * row_live[:, None, :]

    def one_pair(items):
        matrix, amp_block, length = items
        return ladder_term(matrix, amp_block)

    terms = lax.map(one_pair, (matrices, masked, domain_length))
    summed = lax.psum(terms, "virt")
    rows = order // lax.axis_size("virt")
    return lax.dynamic_slice_in_dim(summed, lax.axis_index("virt") * rows, rows, 1)


def solution(mesh):
    placed = (
        P("pair", "virt", None),
        P("virt", "pair", None, None),
        P("pair", None),
        P("pair"),
        P(),
    )
    return jax.shard_map(
        on_device, mesh=mesh, in_specs=placed, out_specs=P("pair", "virt", None), check_vma=False
    )
```

profile of v0, /device:TPU:2, one launch (start us, length us, event | category | flops | bytes accessed | tf_op | source)
XLA Modules:
  0.0 300.7 jit_solution(1592998112843832967)
XLA Ops:
  6.5 0.0 copy-start
  6.5 0.0 all-gather.5.cloned.1.call-start
  6.5 0.7 all-gather.5.cloned.1.call-update
  7.3 0.0 all-gather.3.cloned.1.call-start
  7.3 0.7 all-gather.3.cloned.1.call-update
  8.0 0.0 all-reduce.2.cloned.1.call-start
  8.1 0.7 broadcast_multiply_fusion.1
  8.7 0.8 compare_select_fusion.1
  9.5 0.1 reshape.131
  9.6 0.0 copy-done
  9.6 0.0 copy-start.1
  9.6 0.7 gather_fusion
  10.3 0.1 reshape.130
  10.4 0.0 copy-done.1
  10.4 0.1 compare_convert_fusion
  10.5 0.1 broadcast_bitcast_fusion
  10.6 0.1 broadcast_multiply_fusion
  10.7 36.2 %all-gather.5.cloned.1.call-done = f32[2,512,512]{2,1,0:T(8,128)} async-done(((f32[2,64,512]{2,1,0:T(8,128)}), f32[2,512,512]{2,1,0:T(8,128)}) %all-gather.5.cloned.1.call-update) | async-done | bytes 2097168 | tf_op jit(solution)/shard_map/all_gather | solution.py:18
  46.8 3.2 %multiply_multiply_fusion = f32[2,512,512]{2,1,0:T(8,128)} fusion(f32[2,512,512]{2,1,0:T(8,128)} %all-gather.5.cloned.1.call-done, f32[2,512]{1,0:T(2,128)S(1)} %bitcast.44), kind=kLoop, calls=%fused_computation.13 | loop fusion | flops 1048576 | bytes 4198400 | tf_op jit(solution)/shard_map/mul | solution.py:29
  50.0 145.4 %all-gather.3.cloned.1.call-done = f32[1,64,128,128]{3,2,0,1:T(8,128)} async-done(((f32[1,1,128,128]{3,2,0,1:T(8,128)}), f32[1,64,128,128]{3,2,0,1:T(8,128)}) %all-gather.3.cloned.1.call-update) | async-done | bytes 4194320 | tf_op jit(solution)/shard_map/all_gather | solution.py:19
  195.4 2.9 gather_fusion.1
  198.3 0.3 multiply_bitcast_fusion
  198.6 2.7 copy.9
  201.3 2.1 reshape.128
  203.4 11.9 %while.10 = (s32[]{:T(128)}, f32[2,512,512]{2,1,0:T(8,128)}, f32[2,1,512,512]{3,2,1,0:T(8,128)S(1)}, f32[2,512,512]{2,1,0:T(8,128)}, s32[]{:T(128)}) while((s32[]{:T(128)}, f32[2,512,512]{2,1,0:T(8,128)}, f32[2,1,512,512]{3,2,1,0:T(8,128)S(1)}, f32[2,512,512]{2,1,0:T(8,128)}, s32[]{:T(128)}) %tuple.18), condition=%wide.region_1.2_spmd, body=%wide.region_0.1_spmd.sunk | while | flops 3221225472 | bytes 6293565 | solution.py:35
  203.4 3.1 %fusion.22 = f32[512,512]{1,0:T(8,128)S(1)} fusion(f32[2,512,512]{2,1,0:T(8,128)} %get-tuple-element.74, s32[]{:T(128)} %get-tuple-element.66, f32[2,1,512,512]{3,2,1,0:T(8,128)S(1)} %get-tuple-element.73), kind=kOutput, calls=%fused_computation.4.clone.1 | convolution fusion | flops 1610612736 | bytes 3146752 | tf_op jit(solution)/shard_map/while/body/eval_jaxpr/qrc,cd->qrd/dot_general | solution.py:12
  206.5 2.9 fusion.23
  209.3 3.1 %fusion.22 = f32[512,512]{1,0:T(8,128)S(1)} fusion(f32[2,512,512]{2,1,0:T(8,128)} %get-tuple-element.74, s32[]{:T(128)} %get-tuple-element.66, f32[2,1,512,512]{3,2,1,0:T(8,128)S(1)} %get-tuple-element.73), kind=kOutput, calls=%fused_computation.4.clone.1 | convolution fusion | flops 1610612736 | bytes 3146752 | tf_op jit(solution)/shard_map/while/body/eval_jaxpr/qrc,cd->qrd/dot_general | solution.py:12
  212.4 2.9 fusion.23
  215.3 0.0 all-reduce.2.cloned.1.call-update
  215.3 77.2 %all-reduce.2.cloned.1.call-done = f32[2,512,512]{2,1,0:T(8,128)} async-done(((f32[2,512,512]{2,1,0:T(8,128)}), f32[2,512,512]{2,1,0:T(8,128)}) %all-reduce.2.cloned.1.call-update) | async-done | bytes 2097168 | tf_op jit(solution)/shard_map/psum | solution.py:36
  292.5 1.7 constant_dynamic-slice_fusion
  (6 shorter events, 0.0 us)
Async XLA Ops:
  6.5 3.1 %copy-start = (s32[64]{0:T(128)S(1)}, s32[64]{0:T(128)}, u32[]{:S(2)}) copy-start(s32[64]{0:T(128)} %param.11) | copy-start | bytes 772
  6.5 40.3 %all-gather.5.cloned.1.call-start = ((), (), s32[]{:S(2)}) async-start(), calls=%async_computation.1 | async-start | bytes 2359296 | tf_op jit(solution)/shard_map/all_gather | solution.py:18
  7.3 188.2 %all-gather.3.cloned.1.call-start = ((), (), s32[]{:S(2)}) async-start(), calls=%async_computation | async-start | bytes 4259840 | tf_op jit(solution)/shard_map/all_gather | solution.py:19
  8.0 284.5 %all-reduce.2.cloned.1.call-start = ((), (), s32[]{:S(2)}) async-start(), calls=%async_computation.2 | async-start | bytes 4194304 | tf_op jit(solution)/shard_map/psum | solution.py:36
  9.6 0.8 copy-start.1
Sparse Core Ops, SparseCore 0:
  9.5 37.3 all-gather.4
  49.8 145.5 all-gather.2
  215.4 77.0 all-reduce.1
where the time goes:
time: 301 us
  waiting for transfers between devices  260 us (86%)
  between operations  13.2 us (4%)
  matrix products  11.9 us (4%)
  local copies, waits for them, and re-layouts  10.3 us (3%)
  other arithmetic  5.04 us (2%)
    all_gather x1, waiting for transfers between devices, on_device(): whole_store = lax.all_gather(integral_store, 'pair', axis=1, tiled=True)  145 us
    psum x1, waiting for transfers between devices, on_device(): summed = lax.psum(terms, 'virt')  77.2 us
    all_gather x1, waiting for transfers between devices, on_device(): full_amps = lax.all_gather(amplitudes, 'virt', axis=1, tiled=True)  36.2 us
    dot_general x2, matrix products, ladder_term(): jnp.einsum('qrc,cd->qrd', matrix, masked, precision=lax.Precision.HIGHEST)  6.15 us
  transfers between devices with their start and end apart: 3, of which 3 were waited for; matrix products, arithmetic and copies ran while one was open for 2% of the time, Pallas kernels for 0%

commit v1 on v0

--- a/solution.py
+++ b/solution.py
@@ -15,7 +15,12 @@
 
 def on_device(amplitudes, integral_store, domains, domain_length, owner_map):
     order = M * TILE
-    full_amps = lax.all_gather(amplitudes, "virt", axis=1, tiled=True)
+    ring = [amplitudes]
+    for hop in range(7):
+        ring.append(lax.ppermute(ring[-1], "virt", [(dev, (dev + 1) % 8) for dev in range(8)]))
+    full_amps = jnp.roll(
+        jnp.concatenate(ring[::-1], axis=1), (lax.axis_index("virt") + 1) * ring[0].shape[1], axis=1
+    )
     whole_store = lax.all_gather(integral_store, "pair", axis=1, tiled=True)
     local_q = integral_store.shape[0]
     pairs = amplitudes.shape[0]

time: 301 us -> 266 us (0.88)
  waiting for transfers between devices: 260 us -> 225 us
    ppermute x0 -> x7, waiting for transfers between devices: none -> 46 us  [on_device(): lax.ppermute(ring[-1], 'virt', [(dev, (dev + 1) % 8) for dev in range(8)])]
    all_gather x1, waiting for transfers between devices: 145 us -> 101 us  [on_device(): whole_store = lax.all_gather(integral_store, 'pair', axis=1, tiled=True)]
    all_gather x1 -> x0, waiting for transfers between devices: 36.2 us -> none  [on_device(): full_amps = lax.all_gather(amplitudes, 'virt', axis=1, tiled=True)]
  transfers between devices with their start and end apart: 3 -> 9, of which waited for: 3 -> 9; matrix products, arithmetic and copies ran while one was open for 2% -> 2% of each run, Pallas kernels for 0% -> 0%
where the time goes in v1:
time: 266 us
  waiting for transfers between devices  225 us (85%)
  between operations  13.6 us (5%)
  matrix products  11.9 us (4%)
  local copies, waits for them, and re-layouts  10.6 us (4%)
  other arithmetic  4.11 us (2%)
    all_gather x1, waiting for transfers between devices, on_device(): whole_store = lax.all_gather(integral_store, 'pair', axis=1, tiled=True)  101 us
    psum x1, waiting for transfers between devices, on_device(): summed = lax.psum(terms, 'virt')  77.2 us
    ppermute x7, waiting for transfers between devices, on_device(): lax.ppermute(ring[-1], 'virt', [(dev, (dev + 1) % 8) for dev in range(8)])  46 us
    dot_general x2, matrix products, ladder_term(): jnp.einsum('qrc,cd->qrd', matrix, masked, precision=lax.Precision.HIGHEST)  6.15 us
    dot_general x2, matrix products, ladder_term(): jnp.einsum('qrd,qbd->rb', half, matrix, precision=lax.Precision.HIGHEST)  5.75 us
  transfers between devices with their start and end apart: 9, of which 9 were waited for; matrix products, arithmetic and copies ran while one was open for 2% of the time, Pallas kernels for 0%

profile of v1, /device:TPU:2, one launch (start us, length us, event | category | flops | bytes accessed | tf_op | source)
XLA Modules:
  0.0 265.6 jit_solution(2595661007710129526)
XLA Ops:
  6.5 0.0 copy-start
  6.5 0.0 copy-start.1
  6.5 0.0 all-gather.2.cloned.1.call-start
  6.5 0.7 all-gather.2.cloned.1.call-update
  7.3 0.0 all-reduce.2.cloned.1.call-start
  7.3 0.0 collective-permute-start
  7.3 7.2 %collective-permute-done = f32[2,64,512]{2,1,0:T(8,128)S(1)} collective-permute-done((f32[2,64,512]{2,1,0:T(8,128)}, f32[2,64,512]{2,1,0:T(8,128)S(1)}, u32[]{:S(2)}, u32[]{:S(2)}) %collective-permute-start) | collective-permute-done | bytes 262176 | tf_op jit(solution)/shard_map/ppermute | solution.py:20
  14.5 0.0 collective-permute-start.1
  14.5 7.0 %collective-permute-done.1 = f32[2,64,512]{2,1,0:T(8,128)S(1)} collective-permute-done((f32[2,64,512]{2,1,0:T(8,128)S(1)}, f32[2,64,512]{2,1,0:T(8,128)S(1)}, u32[]{:S(2)}, u32[]{:S(2)}) %collective-permute-start.1) | collective-permute-done | bytes 262176 | tf_op jit(solution)/shard_map/ppermute | solution.py:20
  21.5 0.0 collective-permute-start.2
  21.5 0.7 broadcast_multiply_fusion.1
  22.2 6.3 %collective-permute-done.2 = f32[2,64,512]{2,1,0:T(8,128)S(1)} collective-permute-done((f32[2,64,512]{2,1,0:T(8,128)S(1)}, f32[2,64,512]{2,1,0:T(8,128)S(1)}, u32[]{:S(2)}, u32[]{:S(2)}) %collective-permute-start.2) | collective-permute-done | bytes 262176 | tf_op jit(solution)/shard_map/ppermute | solution.py:20
  28.6 0.0 collective-permute-start.3
  28.6 0.8 compare_select_fusion.1
  29.3 0.1 reshape.131
  29.4 0.7 compare_convert_fusion
  30.1 5.4 %collective-permute-done.3 = f32[2,64,512]{2,1,0:T(8,128)S(1)} collective-permute-done((f32[2,64,512]{2,1,0:T(8,128)S(1)}, f32[2,64,512]{2,1,0:T(8,128)S(1)}, u32[]{:S(2)}, u32[]{:S(2)}) %collective-permute-start.3) | collective-permute-done | bytes 262176 | tf_op jit(solution)/shard_map/ppermute | solution.py:20
  35.6 0.0 collective-permute-start.4
  35.6 0.0 copy-done
  35.6 0.7 gather_fusion
  36.3 0.1 broadcast_bitcast_fusion
  36.4 6.2 %collective-permute-done.4 = f32[2,64,512]{2,1,0:T(8,128)S(1)} collective-permute-done((f32[2,64,512]{2,1,0:T(8,128)S(1)}, f32[2,64,512]{2,1,0:T(8,128)S(1)}, u32[]{:S(2)}, u32[]{:S(2)}) %collective-permute-start.4) | collective-permute-done | bytes 262176 | tf_op jit(solution)/shard_map/ppermute | solution.py:20
  42.6 0.0 collective-permute-start.5
  42.6 0.1 reshape.130
  42.7 6.9 %collective-permute-done.5 = f32[2,64,512]{2,1,0:T(8,128)S(1)} collective-permute-done((f32[2,64,512]{2,1,0:T(8,128)S(1)}, f32[2,64,512]{2,1,0:T(8,128)S(1)}, u32[]{:S(2)}, u32[]{:S(2)}) %collective-permute-start.5) | collective-permute-done | bytes 262176 | tf_op jit(solution)/shard_map/ppermute | solution.py:20
  49.6 0.0 collective-permute-start.6
  49.6 0.1 broadcast_multiply_fusion
  49.7 6.9 %collective-permute-done.6 = f32[2,64,512]{2,1,0:T(8,128)S(1)} collective-permute-done((f32[2,64,512]{2,1,0:T(8,128)S(1)}, f32[2,64,512]{2,1,0:T(8,128)S(1)}, u32[]{:S(2)}, u32[]{:S(2)}) %collective-permute-start.6) | collective-permute-done | bytes 262176 | tf_op jit(solution)/shard_map/ppermute | solution.py:20
  56.8 0.0 copy-done.1
  57.0 1.6 multiply_multiply_fusion
  58.6 101.4 %all-gather.2.cloned.1.call-done = f32[1,64,128,128]{3,2,0,1:T(8,128)} async-done(((f32[1,1,128,128]{3,2,0,1:T(8,128)}), f32[1,64,128,128]{3,2,0,1:T(8,128)}) %all-gather.2.cloned.1.call-update) | async-done | bytes 4194320 | tf_op jit(solution)/shard_map/all_gather | solution.py:24
  160.0 2.9 %gather_fusion.1 = f32[32,128,128]{2,1,0:T(8,128)S(1)} fusion(f32[64,128,128]{2,1,0:T(8,128)} %bitcast.42, s32[1024]{0:T(1024)S(1)} %pad_clamp_fusion), kind=kCustom, calls=%fused_computation.1 | custom fusion | bytes 4194432 | tf_op jit(solution)/shard_map/jit(_take)/gather | solution.py:29
  162.9 0.3 multiply_bitcast_fusion
  163.2 2.7 %copy.9 = f32[2,1,4,128,4,128]{5,4,3,2,0,1:T(4,128)} copy(f32[2,1,4,128,4,128]{5,3,4,2,0,1:T(8,128)S(1)} %multiply_bitcast_fusion) | data formatting | bytes 4194304 | tf_op jit(solution)/shard_map/transpose | solution.py:32
  165.8 2.1 reshape.128
  167.9 11.9 %while.10 = (s32[]{:T(128)}, f32[2,512,512]{2,1,0:T(8,128)}, f32[2,1,512,512]{3,2,1,0:T(8,128)S(1)}, f32[2,512,512]{2,1,0:T(8,128)}, s32[]{:T(128)}) while((s32[]{:T(128)}, f32[2,512,512]{2,1,0:T(8,128)}, f32[2,1,512,512]{3,2,1,0:T(8,128)S(1)}, f32[2,512,512]{2,1,0:T(8,128)}, s32[]{:T(128)}) %tuple.18), condition=%wide.region_1.2_spmd, body=%wide.region_0.1_spmd.sunk | while | flops 3221225472 | bytes 6293565 | solution.py:40
  167.9 3.1 %fusion.22 = f32[512,512]{1,0:T(8,128)S(1)} fusion(f32[2,512,512]{2,1,0:T(8,128)} %get-tuple-element.74, s32[]{:T(128)} %get-tuple-element.66, f32[2,1,512,512]{3,2,1,0:T(8,128)S(1)} %get-tuple-element.73), kind=kOutput, calls=%fused_computation.4.clone.1 | convolution fusion | flops 1610612736 | bytes 3146752 | tf_op jit(solution)/shard_map/while/body/eval_jaxpr/qrc,cd->qrd/dot_general | solution.py:12
  171.0 2.9 %fusion.23 = f32[2,512,512]{2,1,0:T(8,128)} fusion(f32[2,512,512]{2,1,0:T(8,128)} %get-tuple-element.67, s32[]{:T(128)} %get-tuple-element.66, f32[512,512]{1,0:T(8,128)S(1)} %fusion.22, f32[2,1,512,512]{3,2,1,0:T(8,128)S(1)} %get-tuple-element.73), kind=kOutput, calls=%fused_computation.3.clone.1 | convolution fusion | flops 1610612736 | bytes 3146752 | tf_op jit(solution)/shard_map/while/body/eval_jaxpr/qrd,qbd->rb/dot_general | solution.py:13
  173.9 3.1 %fusion.22 = f32[512,512]{1,0:T(8,128)S(1)} fusion(f32[2,512,512]{2,1,0:T(8,128)} %get-tuple-element.74, s32[]{:T(128)} %get-tuple-element.66, f32[2,1,512,512]{3,2,1,0:T(8,128)S(1)} %get-tuple-element.73), kind=kOutput, calls=%fused_computation.4.clone.1 | convolution fusion | flops 1610612736 | bytes 3146752 | tf_op jit(solution)/shard_map/while/body/eval_jaxpr/qrc,cd->qrd/dot_general | solution.py:12
  177.0 2.9 %fusion.23 = f32[2,512,512]{2,1,0:T(8,128)} fusion(f32[2,512,512]{2,1,0:T(8,128)} %get-tuple-element.67, s32[]{:T(128)} %get-tuple-element.66, f32[512,512]{1,0:T(8,128)S(1)} %fusion.22, f32[2,1,512,512]{3,2,1,0:T(8,128)S(1)} %get-tuple-element.73), kind=kOutput, calls=%fused_computation.3.clone.1 | convolution fusion | flops 1610612736 | bytes 3146752 | tf_op jit(solution)/shard_map/while/body/eval_jaxpr/qrd,qbd->rb/dot_general | solution.py:13
  179.9 0.0 all-reduce.2.cloned.1.call-update
  179.9 77.2 %all-reduce.2.cloned.1.call-done = f32[2,512,512]{2,1,0:T(8,128)} async-done(((f32[2,512,512]{2,1,0:T(8,128)}), f32[2,512,512]{2,1,0:T(8,128)}) %all-reduce.2.cloned.1.call-update) | async-done | bytes 2097168 | tf_op jit(solution)/shard_map/psum | solution.py:41
  257.1 1.7 constant_dynamic-slice_fusion
  (22 shorter events, 0.3 us)
Async XLA Ops:
  6.5 29.0 %copy-start = (s32[64]{0:T(128)S(1)}, s32[64]{0:T(128)}, u32[]{:S(2)}) copy-start(s32[64]{0:T(128)} %param.11) | copy-start | bytes 772
  6.5 50.2 %copy-start.1 = (f32[2,64,512]{2,1,0:T(8,128)S(1)}, f32[2,64,512]{2,1,0:T(8,128)}, u32[]{:S(2)}) copy-start(f32[2,64,512]{2,1,0:T(8,128)} %param.7) | copy-start | bytes 786436
  6.5 153.5 %all-gather.2.cloned.1.call-start = ((), (), s32[]{:S(2)}) async-start(), calls=%async_computation | async-start | bytes 4259840 | tf_op jit(solution)/shard_map/all_gather | solution.py:24
  7.3 249.9 %all-reduce.2.cloned.1.call-start = ((), (), s32[]{:S(2)}) async-start(), calls=%async_computation.1 | async-start | bytes 4194304 | tf_op jit(solution)/shard_map/psum | solution.py:41
  7.3 7.2 %collective-permute-start = (f32[2,64,512]{2,1,0:T(8,128)}, f32[2,64,512]{2,1,0:T(8,128)S(1)}, u32[]{:S(2)}, u32[]{:S(2)}) collective-permute-start(f32[2,64,512]{2,1,0:T(8,128)} %param.7), channel_id=1, source_target_pairs={{0,1},{1,2},{2,3},{3,4},{4,5},{5,6},{6,7},{7,0},{8,9},{9,10},{10,1... | collective-permute-start | bytes 786440 | tf_op jit(solution)/shard_map/ppermute | solution.py:20
  14.5 7.0 %collective-permute-start.1 = (f32[2,64,512]{2,1,0:T(8,128)S(1)}, f32[2,64,512]{2,1,0:T(8,128)S(1)}, u32[]{:S(2)}, u32[]{:S(2)}) collective-permute-start(f32[2,64,512]{2,1,0:T(8,128)S(1)} %collective-permute-done), channel_id=1, source_target_pairs={{0,1},{1,2},{2,3},{3,4},{4,5},{5,6},{6,7},{7,0},{8,9},{9,10},{10,1... | collective-permute-start | bytes 786440 | tf_op jit(solution)/shard_map/ppermute | solution.py:20
  21.5 7.0 %collective-permute-start.2 = (f32[2,64,512]{2,1,0:T(8,128)S(1)}, f32[2,64,512]{2,1,0:T(8,128)S(1)}, u32[]{:S(2)}, u32[]{:S(2)}) collective-permute-start(f32[2,64,512]{2,1,0:T(8,128)S(1)} %collective-permute-done.1), channel_id=1, source_target_pairs={{0,1},{1,2},{2,3},{3,4},{4,5},{5,6},{6,7},{7,0},{8,9},{9,10},{10,1... | collective-permute-start | bytes 786440 | tf_op jit(solution)/shard_map/ppermute | solution.py:20
  28.6 7.0 %collective-permute-start.3 = (f32[2,64,512]{2,1,0:T(8,128)S(1)}, f32[2,64,512]{2,1,0:T(8,128)S(1)}, u32[]{:S(2)}, u32[]{:S(2)}) collective-permute-start(f32[2,64,512]{2,1,0:T(8,128)S(1)} %collective-permute-done.2), channel_id=1, source_target_pairs={{0,1},{1,2},{2,3},{3,4},{4,5},{5,6},{6,7},{7,0},{8,9},{9,10},{10,1... | collective-permute-start | bytes 786440 | tf_op jit(solution)/shard_map/ppermute | solution.py:20
  35.6 7.0 %collective-permute-start.4 = (f32[2,64,512]{2,1,0:T(8,128)S(1)}, f32[2,64,512]{2,1,0:T(8,128)S(1)}, u32[]{:S(2)}, u32[]{:S(2)}) collective-permute-start(f32[2,64,512]{2,1,0:T(8,128)S(1)} %collective-permute-done.3), channel_id=1, source_target_pairs={{0,1},{1,2},{2,3},{3,4},{4,5},{5,6},{6,7},{7,0},{8,9},{9,10},{10,1... | collective-permute-start | bytes 786440 | tf_op jit(solution)/shard_map/ppermute | solution.py:20
  42.6 7.0 %collective-permute-start.5 = (f32[2,64,512]{2,1,0:T(8,128)S(1)}, f32[2,64,512]{2,1,0:T(8,128)S(1)}, u32[]{:S(2)}, u32[]{:S(2)}) collective-permute-start(f32[2,64,512]{2,1,0:T(8,128)S(1)} %collective-permute-done.4), channel_id=1, source_target_pairs={{0,1},{1,2},{2,3},{3,4},{4,5},{5,6},{6,7},{7,0},{8,9},{9,10},{10,1... | collective-permute-start | bytes 786440 | tf_op jit(solution)/shard_map/ppermute | solution.py:20
  49.6 7.0 %collective-permute-start.6 = (f32[2,64,512]{2,1,0:T(8,128)S(1)}, f32[2,64,512]{2,1,0:T(8,128)S(1)}, u32[]{:S(2)}, u32[]{:S(2)}) collective-permute-start(f32[2,64,512]{2,1,0:T(8,128)S(1)} %collective-permute-done.5), channel_id=1, source_target_pairs={{0,1},{1,2},{2,3},{3,4},{4,5},{5,6},{6,7},{7,0},{8,9},{9,10},{10,1... | collective-permute-start | bytes 786440 | tf_op jit(solution)/shard_map/ppermute | solution.py:20
Sparse Core Ops, SparseCore 0:
  10.3 149.6 all-gather.1
  180.0 77.0 all-reduce.1
